TPU v7x, 128 devices: a whole 4x4x4 slice. The times are simulated.
128 devices in a mesh: dp: 2 (over x_lo), expert: 64 (over z, x_hi, y, core).
Axes of the slice: x: 4 (x_hi: 2, x_lo: 2; x = x_hi * 2 + x_lo), y: 4, z: 4, core: 2. Of those that a mesh axis runs over, the one named last changes fastest.
Arguments:
- tokens: bfloat16 [32768, 1024], P(('dp', 'expert')), may hold values from -6 to 6
- modulation: bfloat16 [128, 2, 1024], P(('dp', 'expert')), may hold values from -3 to 3
- router_weight: bfloat16 [1024, 64], replicated, may hold values from -0.1875 to 0.1875
- weight_in: bfloat16 [64, 1024, 4096], P('expert', None, 'dp'), may hold values from -0.1875 to 0.1875
- weight_out: bfloat16 [64, 4096, 1024], P('expert', 'dp'), may hold values from -0.09375 to 0.09375
- chosen: int32 [2, 64, 256], P('dp'), may hold values from 0 to 16383, as said below
- grad_out: bfloat16 [32768, 1024], P(('dp', 'expert')), may hold values from -4 to 4
Outputs:
- grad_tokens: bfloat16 [32768, 1024], P(('dp', 'expert'))
- grad_mod: float32 [128, 2, 1024], P(('dp', 'expert'))
- grad_router: float32 [1024, 64], replicated
- grad_weight_in: bfloat16 [64, 1024, 4096], P('expert', None, 'dp')
- grad_weight_out: bfloat16 [64, 4096, 1024], P('expert', 'dp')
Inputs may be any that keep to these rules, and one draw needn't show every extreme that they name: `chosen`: for each slice and expert the 256 positions are distinct; at most 8 of them lie in one image's 256 tokens, and in one image exactly 8.
All inputs are finite; a program needn't handle non-finite values.
Results may differ from a plain program's by a relative error of at most 0.008.
Values may be sent and summed in bfloat16 or wider, within the bound.
A program may use at most 128 MiB of HBM per device.

v0:
```python
import jax
import jax.numpy as jnp
from jax import lax
from jax.sharding import PartitionSpec as P

gelu_root = 0.7978845608028654
gelu_cube = 0.044715
norm_eps = 1e-06


def gelu_value(values):
    inner = gelu_root * (values + gelu_cube * values * values * values)
    return 0.5 * values * (1.0 + jnp.tanh(inner))


def gelu_slope(values):
    tangent = jnp.tanh(gelu_root * (values + gelu_cube * values * values * values))
    return 0.5 * (1.0 + tangent) + 0.5 * values * (1.0 - tangent * tangent) * gelu_root * (
        1.0 + 3.0 * gelu_cube * values * values
    )


def finish_terms(preact, upstream, rows_g, rows_p):
    hidden = gelu_value(preact).astype(jnp.bfloat16)
    score_sum = jnp.sum(hidden.astype(jnp.float32) * upstream, axis=1)
    prob_col = rows_p.astype(jnp.float32)[:, None]
    grad_y = (prob_col * rows_g.astype(jnp.float32)).astype(jnp.bfloat16)
    grad_pre = (prob_col * upstream * gelu_slope(preact)).astype(jnp.bfloat16)
    return (hidden, score_sum, grad_y, grad_pre)


def body(tokens, modulation, router_weight, weight_in, weight_out, chosen, grad_out):
    tok_count = tokens.shape[0]
    model_width = tokens.shape[1]
    experts = lax.axis_size("expert")
    my_index = lax.axis_index("expert")
    most_rows = 2 * tok_count // experts
    x_float = tokens.astype(jnp.float32)
    average = jnp.mean(x_float, axis=1, keepdims=True)
    centred = x_float - average
    spread = jnp.mean(centred * centred, axis=1, keepdims=True)
    inverse = lax.rsqrt(spread + norm_eps)
    normed = centred * inverse
    shift_mod = modulation[0, 0].astype(jnp.float32)
    scale_mod = modulation[0, 1].astype(jnp.float32)
    normal_u = (normed * (1.0 + scale_mod) + shift_mod).astype(jnp.bfloat16)
    gate_prob = jax.nn.sigmoid(
        jnp.dot(normal_u, router_weight, preferred_element_type=jnp.float32)
    ).astype(jnp.bfloat16)
    picked = chosen[0]
    local_row = picked - my_index * tok_count
    is_mine = (local_row >= 0) & (local_row < tok_count)
    list_len = picked.shape[1]
    list_pos = jnp.arange(list_len, dtype=jnp.int32)
    before = (list_pos[:, None] < list_pos[None, :]).astype(jnp.bfloat16)
    rank_in = jnp.dot(
        is_mine.astype(jnp.bfloat16), before, preferred_element_type=jnp.float32
    ).astype(jnp.int32)
    slot_at = jnp.where(is_mine, rank_in, most_rows)
    expert_col = jnp.arange(experts, dtype=jnp.int32)[:, None]
    rows_idx = (
        jnp.full((experts, most_rows), tok_count, jnp.int32)
        .at[expert_col, slot_at]
        .set(local_row, mode="drop")
    )
    u_pad = jnp.concatenate([normal_u, jnp.zeros((1, model_width), jnp.bfloat16)], axis=0)
    g_pad = jnp.concatenate([grad_out, jnp.zeros((1, model_width), jnp.bfloat16)], axis=0)
    p_pad = jnp.concatenate([gate_prob, jnp.zeros((1, experts), jnp.bfloat16)], axis=0)
    u_send = u_pad[rows_idx]
    g_send = g_pad[rows_idx]
    p_send = p_pad[rows_idx, expert_col]
    u_recv, g_recv, p_recv = (
        lax.all_to_all(u_send, "expert", split_axis=0, concat_axis=0, tiled=True),
        lax.all_to_all(g_send, "expert", split_axis=0, concat_axis=0, tiled=True),
        lax.all_to_all(p_send, "expert", split_axis=0, concat_axis=0, tiled=True),
    )
    u_all, g_all, p_all = (
        lax.all_gather(u_recv, "dp", axis=0, tiled=True),
        lax.all_gather(g_recv, "dp", axis=0, tiled=True),
        lax.all_gather(p_recv, "dp", axis=0, tiled=True),
    )
    rows_u = u_all.reshape(-1, model_width)
    rows_g = g_all.reshape(-1, model_width)
    rows_p = p_all.reshape(-1)
    first_w = weight_in[0]
    second_w = weight_out[0]
    preact = jnp.dot(rows_u, first_w, preferred_element_type=jnp.float32)
    upstream = lax.dot_general(
        rows_g, second_w, (((1,), (1,)), ((), ())), preferred_element_type=jnp.float32
    )
    hidden, score_sum, grad_y, grad_pre = finish_terms(preact, upstream, rows_g, rows_p)
    grad_first = lax.dot_general(
        rows_u, grad_pre, (((0,), (0,)), ((), ())), preferred_element_type=jnp.float32
    )
    grad_second = lax.dot_general(
        hidden, grad_y, (((0,), (0,)), ((), ())), preferred_element_type=jnp.float32
    )
    rows_part = lax.dot_general(
        grad_pre, first_w, (((1,), (1,)), ((), ())), preferred_element_type=jnp.float32
    )
    grad_sum, score_total = (
        lax.psum_scatter(
            rows_part.reshape(-1, most_rows, model_width), "dp", scatter_dimension=0, tiled=True
        ),
        lax.psum_scatter(score_sum.reshape(-1, most_rows), "dp", scatter_dimension=0, tiled=True),
    )
    grad_weight_in = grad_first.astype(jnp.bfloat16)[None]
    grad_weight_out = grad_second.astype(jnp.bfloat16)[None]
    grad_back = grad_sum.astype(jnp.bfloat16)
    score_back = score_total.astype(jnp.bfloat16)
    grad_ret, score_ret = (
        lax.all_to_all(grad_back, "expert", split_axis=0, concat_axis=0, tiled=True),
        lax.all_to_all(score_back, "expert", split_axis=0, concat_axis=0, tiled=True),
    )
    grad_u = (
        jnp.zeros((tok_count + 1, model_width), jnp.float32)
        .at[rows_idx]
        .add(grad_ret.astype(jnp.float32))[:tok_count]
    )
    prob_sent = p_send.astype(jnp.float32)
    logit_terms = score_ret.astype(jnp.float32) * prob_sent * (1.0 - prob_sent)
    grad_logit = (
        jnp.zeros((tok_count + 1, experts), jnp.float32)
        .at[rows_idx, expert_col]
        .add(logit_terms)[:tok_count]
    )
    grad_u = grad_u + jnp.dot(
        grad_logit, router_weight.astype(jnp.float32).T, precision=lax.Precision.HIGHEST
    )
    router_term = jnp.dot(
        normal_u.astype(jnp.float32).T, grad_logit, precision=lax.Precision.HIGHEST
    )
    grad_router = lax.psum(router_term, ("dp", "expert"))
    grad_shift = jnp.sum(grad_u, axis=0)
    grad_scale = jnp.sum(grad_u * normed, axis=0)
    grad_mod = jnp.stack([grad_shift, grad_scale], axis=0)[None]
    grad_norm = grad_u * (1.0 + scale_mod)
    centre_term = jnp.mean(grad_norm, axis=1, keepdims=True)
    slope_term = jnp.mean(grad_norm * normed, axis=1, keepdims=True)
    grad_tokens = (
        grad_out.astype(jnp.float32) + (grad_norm - centre_term - normed * slope_term) * inverse
    ).astype(jnp.bfloat16)
    return (grad_tokens, grad_mod, grad_router, grad_weight_in, grad_weight_out)


def solution(mesh):
    placed = (
        P(("dp", "expert"), None),
        P(("dp", "expert"), None, None),
        P(),
        P("expert", None, "dp"),
        P("expert", "dp", None),
        P("dp", None, None),
        P(("dp", "expert"), None),
    )
    return jax.shard_map(
        body,
        mesh=mesh,
        in_specs=placed,
        out_specs=(
            P(("dp", "expert"), None),
            P(("dp", "expert"), None, None),
            P(),
            P("expert", None, "dp"),
            P("expert", "dp", None),
        ),
        check_vma=False,
    )
```

profile of v0, /device:TPU:1, one launch (start us, length us, event | category | flops | bytes accessed | tf_op | source)
XLA Modules:
  0.0 482.4 jit_solution(4987873080595867684)
XLA Ops:
  8.6 1.1 fusion.43
  9.7 0.8 subtract_bitcast_fusion
  10.6 1.2 convert_reduce_fusion
  11.8 1.3 fusion.40
  14.7 60.3 %scatter_custom_fusion.2 = s32[512]{0:T(512)S(1)} fusion(s32[16384]{0:T(1024)S(1)} %bitcast.88, s32[16384]{0:T(1024)S(1)} %bitcast.87, s32[]{:T(128)} %constant.15.clone.1), kind=kCustom, calls=%fused_computation.98 | custom fusion | bytes 2052
  75.3 1.3 fusion.33
  76.7 2.1 gather_fusion.2
  78.8 31.8 %all_to_all.37 = bf16[64,8,1024]{2,1,0:T(8,128)(2,1)} all-to-all(bf16[64,8,1024]{2,1,0:T(8,128)(2,1)S(1)} %bitcast.86), channel_id=1, replica_groups=mesh['dp'=2,'expert'=64] {'expert'}, dimensions={0} | all-to-all | bytes 2097152 | tf_op jit(solution)/shard_map/all_to_all | solution.py:73
  110.7 2.1 gather_fusion.1
  112.8 35.0 %all_to_all.38 = bf16[64,8,1024]{2,1,0:T(8,128)(2,1)} all-to-all(bf16[64,8,1024]{2,1,0:T(8,128)(2,1)S(1)} %bitcast.85), channel_id=1, replica_groups=mesh['dp'=2,'expert'=64] {'expert'}, dimensions={0} | all-to-all | bytes 2097152 | tf_op jit(solution)/shard_map/all_to_all | solution.py:74
  148.4 4.9 %gather_fusion = bf16[512]{0:T(512)(128)(2,1)S(1)} fusion(bf16[257,64]{0,1:T(8,128)(2,1)S(1)} %concatenate.17, s32[512]{0:T(512)S(1)} %reshape.85), kind=kCustom, calls=%fused_computation | custom fusion | bytes 6144 | tf_op jit(solution)/shard_map/gather | solution.py:71
  153.4 13.5 %all_to_all.39 = bf16[64,1,8]{2,1,0:T(2,128)(2,1)S(1)} all-to-all(bf16[64,1,8]{2,1,0:T(2,128)(2,1)S(1)} %all_to_all.31), channel_id=1, replica_groups=mesh['dp'=2,'expert'=64] {'expert'}, dimensions={0} | all-to-all | bytes 2048 | tf_op jit(solution)/shard_map/all_to_all | solution.py:75
  166.9 4.7 all-gather
  171.9 10.5 %fusion.9 = f32[1024,2048]{1,0:T(8,128)} fusion(bf16[1,1024,2048]{2,1,0:T(8,128)(2,1)} %param.10, bf16[128,8,1024]{2,1,0:T(8,128)(2,1)} %all-gather.6.cloned.1.call-done), kind=kOutput, calls=%fused_computation.19 | convolution fusion | flops 4294967296 | bytes 14680064 | tf_op jit(solution)/shard_map/dot_general | solution.py:87
  182.4 9.6 %all-gather.4.cloned.1.call-done = bf16[128,8,1024]{2,1,0:T(8,128)(2,1)} async-done(((bf16[64,8,1024]{2,1,0:T(8,128)(2,1)}), bf16[128,8,1024]{2,1,0:T(8,128)(2,1)}) %all-gather.4.cloned.1.call-update) | async-done | bytes 2097168 | tf_op jit(solution)/shard_map/all_gather | solution.py:79
  192.1 14.5 %multiply_reduce_fusion = (f32[1024]{0:T(1024)S(1)}, bf16[1024,2048]{1,0:T(8,128)(2,1)}) fusion(f32[1024,2048]{1,0:T(8,128)} %fusion.9, f32[1024]{0:T(1024)S(1)} %reshape.83, bf16[1,2048,1024]{2,1,0:T(8,128)(2,1)} %param.11, bf16[128,8,1024]{2,1,0:T(8,128)(2,1)} %all-gather.4.cloned.1.call-done), kind=kOutput, calls=%fused_computation.15 | convolution fusion | flops 4347395072 | bytes 18882560 | tf_op jit(solution)/shard_map/dot_general | solution.py:88
  207.8 12.7 %fusion.7 = f32[128,8,1024]{2,0,1:T(8,128)} fusion(bf16[1,1024,2048]{2,1,0:T(8,128)(2,1)} %param.10, bf16[128,8,2048]{2,1,0:T(8,128)(2,1)} %bitcast.95), kind=kOutput, calls=%fused_computation.17 | convolution fusion | flops 4294967296 | bytes 12582912 | tf_op jit(solution)/shard_map/dot_general | solution.py:98
  220.8 0.8 convert_bitcast_fusion.2
  222.2 9.8 %all-to-all-start.4 = ((bf16[64,1,8]{2,1,0:T(2,128)(2,1)}), bf16[64,1,8]{2,1,0:T(2,128)(2,1)S(1)}, u32[]{:S(2)}, u32[]{:S(2)}) async-start(bf16[64,1,8]{2,1,0:T(2,128)(2,1)} %copy.34), calls=%async_computation.6 | async-start | bytes 65536 | tf_op jit(solution)/shard_map/all_to_all | solution.py:113
  232.0 12.8 %convert_bitcast_fusion = bf16[1,2048,1024]{2,1,0:T(8,128)(2,1)} fusion(bf16[128,8,1024]{2,1,0:T(8,128)(2,1)} %all-gather.4.cloned.1.call-done, f32[1024]{0:T(1024)S(1)} %reshape.83, f32[1024,2048]{1,0:T(8,128)} %fusion.9), kind=kOutput, calls=%fused_computation.24 | convolution fusion | flops 4319084544 | bytes 14684160 | tf_op jit(solution)/shard_map/dot_general | solution.py:95
  244.9 35.8 %reduce-scatter.3.cloned.1.call-done = f32[64,8,1024]{2,0,1:T(8,128)} async-done(((f32[128,8,1024]{2,0,1:T(8,128)}), f32[64,8,1024]{2,0,1:T(8,128)}) %reduce-scatter.3.cloned.1.call-update) | async-done | bytes 2097168 | tf_op jit(solution)/shard_map/reduce_scatter | solution.py:102
  280.7 1.7 convert_element_type.100
  282.5 1.6 copy.32
  284.0 10.3 %all-to-all-start.3 = ((bf16[64,8,1024]{2,1,0:T(8,128)(2,1)}), bf16[64,8,1024]{2,1,0:T(8,128)(2,1)S(1)}, u32[]{:S(2)}, u32[]{:S(2)}) async-start(bf16[64,8,1024]{2,1,0:T(8,128)(2,1)} %copy.32), calls=%async_computation.4 | async-start | bytes 2097152 | tf_op jit(solution)/shard_map/all_to_all | solution.py:112
  294.6 9.4 %convert_bitcast_fusion.1 = bf16[1,1024,2048]{2,1,0:T(8,128)(2,1)} fusion(bf16[1024,2048]{1,0:T(8,128)(2,1)} %get-tuple-element.10, bf16[128,8,1024]{2,1,0:T(8,128)(2,1)} %all-gather.6.cloned.1.call-done), kind=kOutput, calls=%fused_computation.26 | convolution fusion | flops 4297064448 | bytes 10485760 | tf_op jit(solution)/shard_map/dot_general | solution.py:92
  304.2 25.8 %scatter_fusion = f32[257,64]{0,1:T(8,128)S(1)} fusion(f32[257,64]{0,1:T(8,128)S(1)} %broadcast_in_dim.31, s32[512]{0:T(512)S(1)} %reshape.115, f32[512]{0:T(512)S(1)} %reshape.117), kind=kCustom, calls=%fused_computation.4 | custom fusion | flops 512 | bytes 10240 | tf_op jit(solution)/shard_map/scatter-add | solution.py:125
  330.0 1.1 fusion.48
  331.1 5.8 %scatter_custom_fusion = f32[257,1024]{1,0:T(8,128)} fusion(s32[512]{0:T(512)S(1)} %reshape.109, bf16[64,8,1024]{2,1,0:T(8,128)(2,1)S(1)} %all-to-all-done.3, f32[]{:T(128)} %constant.14.clone.1), kind=kCustom, calls=%fused_computation.27 | custom fusion | flops 1048576 | bytes 2101252 | tf_op jit(solution)/shard_map/scatter-add | solution.py:118
  336.9 2.3 fusion.39
  339.3 1.2 fusion.38
  341.1 132.8 %all-reduce.5.cloned.1.call-done = f32[1024,64]{0,1:T(8,128)} async-done(((f32[1024,64]{0,1:T(8,128)}), f32[1024,64]{0,1:T(8,128)}) %all-reduce.5.cloned.1.call-update) | async-done | bytes 262160 | tf_op jit(solution)/shard_map/psum | solution.py:133
  474.0 1.7 copy.43
  (55 shorter events, 7.7 us)
Async XLA Ops:
  7.2 140.9 %copy-start = (bf16[1024,64]{0,1:T(8,128)(2,1)S(1)}, bf16[1024,64]{0,1:T(8,128)(2,1)}, u32[]{:S(2)}) copy-start(bf16[1024,64]{0,1:T(8,128)(2,1)} %param.9) | copy-start | bytes 393220
  7.2 164.7 %all-gather.6.cloned.1.call-start = ((), (), s32[]{:S(2)}) async-start(), calls=%async_computation.8 | async-start | bytes 3145728 | tf_op jit(solution)/shard_map/all_gather | solution.py:78
  76.7 34.0 %copy-start.2 = (bf16[256,1024]{1,0:T(8,128)(2,1)S(1)}, bf16[256,1024]{1,0:T(8,128)(2,1)}, u32[]{:S(2)}) copy-start(bf16[256,1024]{1,0:T(8,128)(2,1)} %param.13) | copy-start | bytes 1572868
  110.6 81.5 %all-gather.4.cloned.1.call-start = ((), (), s32[]{:S(2)}) async-start(), calls=%async_computation.7 | async-start | bytes 3145728 | tf_op jit(solution)/shard_map/all_gather | solution.py:79
  147.8 73.0 %reduce-scatter.5.cloned.1.call-start = ((), (), s32[]{:S(2)}) async-start(), calls=%async_computation.10 | async-start | bytes 98304 | tf_op jit(solution)/shard_map/reduce_scatter | solution.py:105
  207.3 73.4 %reduce-scatter.3.cloned.1.call-start = ((), (), s32[]{:S(2)}) async-start(), calls=%async_computation.9 | async-start | bytes 6291456 | tf_op jit(solution)/shard_map/reduce_scatter | solution.py:102
  222.2 61.8 %all-to-all-start.4 = ((bf16[64,1,8]{2,1,0:T(2,128)(2,1)}), bf16[64,1,8]{2,1,0:T(2,128)(2,1)S(1)}, u32[]{:S(2)}, u32[]{:S(2)}) async-start(bf16[64,1,8]{2,1,0:T(2,128)(2,1)} %copy.34), calls=%async_computation.6 | async-start | bytes 65536 | tf_op jit(solution)/shard_map/all_to_all | solution.py:113
  284.0 47.1 %all-to-all-start.3 = ((bf16[64,8,1024]{2,1,0:T(8,128)(2,1)}), bf16[64,8,1024]{2,1,0:T(8,128)(2,1)S(1)}, u32[]{:S(2)}, u32[]{:S(2)}) async-start(bf16[64,8,1024]{2,1,0:T(8,128)(2,1)} %copy.32), calls=%async_computation.4 | async-start | bytes 2097152 | tf_op jit(solution)/shard_map/all_to_all | solution.py:112
  294.4 179.6 %all-reduce.5.cloned.1.call-start = ((), (), s32[]{:S(2)}) async-start(), calls=%async_computation.11 | async-start | bytes 524288 | tf_op jit(solution)/shard_map/psum | solution.py:133
  304.2 32.8 %copy-start.1 = (bf16[256,1024]{1,0:T(8,128)(2,1)S(1)}, bf16[256,1024]{1,0:T(8,128)(2,1)}, u32[]{:S(2)}) copy-start(bf16[256,1024]{1,0:T(8,128)(2,1)} %param.7) | copy-start | bytes 1572868
Sparse Core Ops, SparseCore 0:
  110.7 41.7 all-gather.5
  154.2 37.8 all-gather.3
  207.4 12.1 reduce-scatter.4
  222.4 58.2 reduce-scatter.2
  331.2 142.6 all-reduce.4
where the time goes:
time: 489 us; the launch traced here: 482 us
  waiting for transfers between devices  178 us (36%)
  blocking collectives  85 us (17%)
  local copies, waits for them, and re-layouts  75.1 us (15%)
  matrix products  64.7 us (13%)
  other arithmetic  43.8 us (9%)
  starting transfers between devices  21.1 us (4%)
  between operations  14.3 us (3%)
    psum x1, waiting for transfers between devices, body(): grad_router = lax.psum(router_term, ('dp', 'expert'))  133 us
    unnamed x11, local copies, waits for them, and re-layouts  62.1 us
    reduce_scatter x1, waiting for transfers between devices, body(): lax.psum_scatter(rows_part.reshape(-1, most_rows, model_width), 'dp', sca...  35.8 us
    all_to_all x1, blocking collectives, body(): lax.all_to_all(g_send, 'expert', split_axis=0, concat_axis=0, tiled=True)  35 us
    all_to_all x1, blocking collectives, body(): lax.all_to_all(u_send, 'expert', split_axis=0, concat_axis=0, tiled=True)  31.8 us
    scatter-add x1, other arithmetic, body(): grad_logit = jnp.zeros((tok_count + 1, experts), jnp.float32).at[rows_idx...  25.8 us
    dot_general x1, matrix products, body(): lax.dot_general(rows_g, second_w, (((1,), (1,)), ((), ())), preferred_ele...  14.5 us
    all_to_all x1, blocking collectives, body(): lax.all_to_all(p_send, 'expert', split_axis=0, concat_axis=0, tiled=True)  13.5 us
  transfers between devices with their start and end apart: 7, of which 3 were waited for; matrix products, arithmetic and copies ran while one was open for 20% of the time, Pallas kernels for 0%

commit v1 on v0

--- a/solution.py
+++ b/solution.py
@@ -130,7 +130,7 @@
     router_term = jnp.dot(
         normal_u.astype(jnp.float32).T, grad_logit, precision=lax.Precision.HIGHEST
     )
-    grad_router = lax.psum(router_term, ("dp", "expert"))
+    grad_router = lax.psum(lax.psum(router_term, "expert"), "dp")
     grad_shift = jnp.sum(grad_u, axis=0)
     grad_scale = jnp.sum(grad_u * normed, axis=0)
     grad_mod = jnp.stack([grad_shift, grad_scale], axis=0)[None]

time: 489 us -> 934 us (1.91)
  waiting for transfers between devices: 178 us -> 626 us
    psum x1 -> x2, waiting for transfers between devices: 133 us -> 606 us  [body(): grad_router = lax.psum(lax.psum(router_term, 'expert'), 'dp')]
    reduce_scatter x1, waiting for transfers between devices: 35.8 us -> 10.4 us  [body(): lax.psum_scatter(rows_part.reshape(-1, most_rows, model_width), 'dp', sca...]
    unnamed x11 -> x13, local copies, waits for them, and re-layouts: 62.1 us -> 62.1 us
  transfers between devices with their start and end apart: 7 -> 8, of which waited for: 3 -> 4; matrix products, arithmetic and copies ran while one was open for 20% -> 10% of each run, Pallas kernels for 0% -> 0%
where the time goes in v1:
time: 934 us; the launch traced here: 928 us
  waiting for transfers between devices  626 us (67%)
  blocking collectives  85 us (9%)
  local copies, waits for them, and re-layouts  75.1 us (8%)
  matrix products  62.9 us (7%)
  other arithmetic  43.3 us (5%)
  starting transfers between devices  21.2 us (2%)
  between operations  14.6 us (2%)
    psum x2, waiting for transfers between devices, body(): grad_router = lax.psum(lax.psum(router_term, 'expert'), 'dp')  606 us
    unnamed x13, local copies, waits for them, and re-layouts  62.1 us
    all_to_all x1, blocking collectives, body(): lax.all_to_all(g_send, 'expert', split_axis=0, concat_axis=0, tiled=True)  35 us
    all_to_all x1, blocking collectives, body(): lax.all_to_all(u_send, 'expert', split_axis=0, concat_axis=0, tiled=True)  31.8 us
    scatter-add x1, other arithmetic, body(): grad_logit = jnp.zeros((tok_count + 1, experts), jnp.float32).at[rows_idx...  25.8 us
  transfers between devices with their start and end apart: 8, of which 4 were waited for; matrix products, arithmetic and copies ran while one was open for 10% of the time, Pallas kernels for 0%

profile of v1, /device:TPU:1, one launch (start us, length us, event | category | flops | bytes accessed | tf_op | source)
XLA Modules:
  0.0 927.8 jit_solution(13150576225068640236)
XLA Ops:
  8.6 1.1 fusion.43
  10.6 1.2 convert_reduce_fusion
  11.8 1.3 fusion.40
  14.7 60.3 %scatter_custom_fusion.2 = s32[512]{0:T(512)S(1)} fusion(s32[16384]{0:T(1024)S(1)} %bitcast.88, s32[16384]{0:T(1024)S(1)} %bitcast.87, s32[]{:T(128)} %constant.15.clone.1), kind=kCustom, calls=%fused_computation.98 | custom fusion | bytes 2052
  75.3 1.3 fusion.33
  76.7 2.1 gather_fusion.2
  78.8 31.8 %all_to_all.37 = bf16[64,8,1024]{2,1,0:T(8,128)(2,1)} all-to-all(bf16[64,8,1024]{2,1,0:T(8,128)(2,1)S(1)} %bitcast.86), channel_id=1, replica_groups=mesh['dp'=2,'expert'=64] {'expert'}, dimensions={0} | all-to-all | bytes 2097152 | tf_op jit(solution)/shard_map/all_to_all | solution.py:73
  110.7 2.1 gather_fusion.1
  112.8 35.0 %all_to_all.38 = bf16[64,8,1024]{2,1,0:T(8,128)(2,1)} all-to-all(bf16[64,8,1024]{2,1,0:T(8,128)(2,1)S(1)} %bitcast.85), channel_id=1, replica_groups=mesh['dp'=2,'expert'=64] {'expert'}, dimensions={0} | all-to-all | bytes 2097152 | tf_op jit(solution)/shard_map/all_to_all | solution.py:74
  148.4 4.9 gather_fusion
  153.4 13.5 %all_to_all.39 = bf16[64,1,8]{2,1,0:T(2,128)(2,1)S(1)} all-to-all(bf16[64,1,8]{2,1,0:T(2,128)(2,1)S(1)} %all_to_all.31), channel_id=1, replica_groups=mesh['dp'=2,'expert'=64] {'expert'}, dimensions={0} | all-to-all | bytes 2048 | tf_op jit(solution)/shard_map/all_to_all | solution.py:75
  166.9 4.7 all-gather
  171.9 10.5 %fusion.9 = f32[1024,2048]{1,0:T(8,128)} fusion(bf16[1,1024,2048]{2,1,0:T(8,128)(2,1)} %param.10, bf16[128,8,1024]{2,1,0:T(8,128)(2,1)} %all-gather.6.cloned.1.call-done), kind=kOutput, calls=%fused_computation.19 | convolution fusion | flops 4294967296 | bytes 14680064 | tf_op jit(solution)/shard_map/dot_general | solution.py:87
  182.4 9.6 %all-gather.4.cloned.1.call-done = bf16[128,8,1024]{2,1,0:T(8,128)(2,1)} async-done(((bf16[64,8,1024]{2,1,0:T(8,128)(2,1)}), bf16[128,8,1024]{2,1,0:T(8,128)(2,1)}) %all-gather.4.cloned.1.call-update) | async-done | bytes 2097168 | tf_op jit(solution)/shard_map/all_gather | solution.py:79
  192.1 14.5 %multiply_reduce_fusion = (f32[1024]{0:T(1024)S(1)}, bf16[1024,2048]{1,0:T(8,128)(2,1)}) fusion(f32[1024,2048]{1,0:T(8,128)} %fusion.9, f32[1024]{0:T(1024)S(1)} %reshape.83, bf16[1,2048,1024]{2,1,0:T(8,128)(2,1)} %param.11, bf16[128,8,1024]{2,1,0:T(8,128)(2,1)} %all-gather.4.cloned.1.call-done), kind=kOutput, calls=%fused_computation.15 | convolution fusion | flops 4347395072 | bytes 18882560 | tf_op jit(solution)/shard_map/dot_general | solution.py:88
  207.8 12.7 %fusion.7 = f32[128,8,1024]{2,0,1:T(8,128)} fusion(bf16[1,1024,2048]{2,1,0:T(8,128)(2,1)} %param.10, bf16[128,8,2048]{2,1,0:T(8,128)(2,1)} %bitcast.95), kind=kOutput, calls=%fused_computation.17 | convolution fusion | flops 4294967296 | bytes 12582912 | tf_op jit(solution)/shard_map/dot_general | solution.py:98
  220.8 0.9 convert_bitcast_fusion.2
  222.4 9.8 %all-to-all-start.4 = ((bf16[64,1,8]{2,1,0:T(2,128)(2,1)}), bf16[64,1,8]{2,1,0:T(2,128)(2,1)S(1)}, u32[]{:S(2)}, u32[]{:S(2)}) async-start(bf16[64,1,8]{2,1,0:T(2,128)(2,1)} %copy.34), calls=%async_computation.6 | async-start | bytes 65536 | tf_op jit(solution)/shard_map/all_to_all | solution.py:113
  232.2 12.2 %convert_bitcast_fusion = bf16[1,2048,1024]{2,1,0:T(8,128)(2,1)} fusion(bf16[128,8,1024]{2,1,0:T(8,128)(2,1)S(1)} %copy-done.3, f32[1024]{0:T(1024)S(1)} %reshape.83, f32[1024,2048]{1,0:T(8,128)} %fusion.9), kind=kOutput, calls=%fused_computation.24 | convolution fusion | flops 4319084544 | bytes 14684160 | tf_op jit(solution)/shard_map/dot_general | solution.py:95
  244.5 25.8 %scatter_fusion = f32[257,64]{0,1:T(8,128)S(1)} fusion(f32[257,64]{0,1:T(8,128)S(1)} %broadcast_in_dim.31, s32[512]{0:T(512)S(1)} %reshape.115, f32[512]{0:T(512)S(1)} %reshape.117), kind=kCustom, calls=%fused_computation.4 | custom fusion | flops 512 | bytes 10240 | tf_op jit(solution)/shard_map/scatter-add | solution.py:125
  270.4 10.4 %reduce-scatter.3.cloned.1.call-done = f32[64,8,1024]{2,0,1:T(8,128)} async-done(((f32[128,8,1024]{2,0,1:T(8,128)}), f32[64,8,1024]{2,0,1:T(8,128)}) %reduce-scatter.3.cloned.1.call-update) | async-done | bytes 2097168 | tf_op jit(solution)/shard_map/reduce_scatter | solution.py:102
  280.7 1.7 convert_element_type.100
  282.5 1.6 copy.32
  284.0 10.4 %all-to-all-start.3 = ((bf16[64,8,1024]{2,1,0:T(8,128)(2,1)}), bf16[64,8,1024]{2,1,0:T(8,128)(2,1)S(1)}, u32[]{:S(2)}, u32[]{:S(2)}) async-start(bf16[64,8,1024]{2,1,0:T(8,128)(2,1)} %copy.32), calls=%async_computation.4 | async-start | bytes 2097152 | tf_op jit(solution)/shard_map/all_to_all | solution.py:112
  294.5 1.1 fusion.48
  295.9 9.4 %convert_bitcast_fusion.1 = bf16[1,1024,2048]{2,1,0:T(8,128)(2,1)} fusion(bf16[1024,2048]{1,0:T(8,128)(2,1)} %get-tuple-element.10, bf16[128,8,1024]{2,1,0:T(8,128)(2,1)} %all-gather.6.cloned.1.call-done), kind=kOutput, calls=%fused_computation.26 | convolution fusion | flops 4297064448 | bytes 10485760 | tf_op jit(solution)/shard_map/dot_general | solution.py:92
  305.3 583.0 %all-reduce.6.cloned.1.call-done = f32[1024,64]{0,1:T(8,128)} async-done(((f32[1024,64]{0,1:T(8,128)}), f32[1024,64]{0,1:T(8,128)}) %all-reduce.6.cloned.1.call-update) | async-done | bytes 262160 | tf_op jit(solution)/shard_map/psum | solution.py:133
  888.4 5.1 scatter_custom_fusion
  893.4 1.1 fusion.39
  895.2 1.3 fusion.38
  896.5 22.7 %all-reduce.8.cloned.1.call-done = f32[1024,64]{0,1:T(8,128)} async-done(((f32[1024,64]{0,1:T(8,128)}), f32[1024,64]{0,1:T(8,128)}) %all-reduce.8.cloned.1.call-update) | async-done | bytes 262160 | tf_op jit(solution)/shard_map/psum | solution.py:133
  919.1 1.7 copy.44
  (60 shorter events, 8.6 us)
Async XLA Ops:
  7.2 140.9 %copy-start = (bf16[1024,64]{0,1:T(8,128)(2,1)S(1)}, bf16[1024,64]{0,1:T(8,128)(2,1)}, u32[]{:S(2)}) copy-start(bf16[1024,64]{0,1:T(8,128)(2,1)} %param.9) | copy-start | bytes 393220
  7.2 164.7 %all-gather.6.cloned.1.call-start = ((), (), s32[]{:S(2)}) async-start(), calls=%async_computation.8 | async-start | bytes 3145728 | tf_op jit(solution)/shard_map/all_gather | solution.py:78
  76.7 34.0 %copy-start.2 = (bf16[256,1024]{1,0:T(8,128)(2,1)S(1)}, bf16[256,1024]{1,0:T(8,128)(2,1)}, u32[]{:S(2)}) copy-start(bf16[256,1024]{1,0:T(8,128)(2,1)} %param.13) | copy-start | bytes 1572868
  110.6 81.5 %all-gather.4.cloned.1.call-start = ((), (), s32[]{:S(2)}) async-start(), calls=%async_computation.7 | async-start | bytes 3145728 | tf_op jit(solution)/shard_map/all_gather | solution.py:79
  147.8 73.0 %reduce-scatter.5.cloned.1.call-start = ((), (), s32[]{:S(2)}) async-start(), calls=%async_computation.10 | async-start | bytes 98304 | tf_op jit(solution)/shard_map/reduce_scatter | solution.py:105
  207.3 73.4 %reduce-scatter.3.cloned.1.call-start = ((), (), s32[]{:S(2)}) async-start(), calls=%async_computation.9 | async-start | bytes 6291456 | tf_op jit(solution)/shard_map/reduce_scatter | solution.py:102
  220.5 11.7 %copy-start.3 = (bf16[128,8,1024]{2,1,0:T(8,128)(2,1)S(1)}, bf16[128,8,1024]{2,1,0:T(8,128)(2,1)}, u32[]{:S(2)}) copy-start(bf16[128,8,1024]{2,1,0:T(8,128)(2,1)} %all-gather.4.cloned.1.call-done) | copy-start | bytes 6291460
  222.4 22.0 %all-to-all-start.4 = ((bf16[64,1,8]{2,1,0:T(2,128)(2,1)}), bf16[64,1,8]{2,1,0:T(2,128)(2,1)S(1)}, u32[]{:S(2)}, u32[]{:S(2)}) async-start(bf16[64,1,8]{2,1,0:T(2,128)(2,1)} %copy.34), calls=%async_computation.6 | async-start | bytes 65536 | tf_op jit(solution)/shard_map/all_to_all | solution.py:113
  284.0 604.3 %all-to-all-start.3 = ((bf16[64,8,1024]{2,1,0:T(8,128)(2,1)}), bf16[64,8,1024]{2,1,0:T(8,128)(2,1)S(1)}, u32[]{:S(2)}, u32[]{:S(2)}) async-start(bf16[64,8,1024]{2,1,0:T(8,128)(2,1)} %copy.32), calls=%async_computation.4 | async-start | bytes 2097152 | tf_op jit(solution)/shard_map/all_to_all | solution.py:112
  294.4 593.9 %all-reduce.6.cloned.1.call-start = ((), (), s32[]{:S(2)}) async-start(), calls=%async_computation.11 | async-start | bytes 524288 | tf_op jit(solution)/shard_map/psum | solution.py:133
  295.6 597.8 %copy-start.1 = (bf16[256,1024]{1,0:T(8,128)(2,1)S(1)}, bf16[256,1024]{1,0:T(8,128)(2,1)}, u32[]{:S(2)}) copy-start(bf16[256,1024]{1,0:T(8,128)(2,1)} %param.7) | copy-start | bytes 1572868
  295.6 623.5 %all-reduce.8.cloned.1.call-start = ((), (), s32[]{:S(2)}) async-start(), calls=%async_computation.12 | async-start | bytes 524288 | tf_op jit(solution)/shard_map/psum | solution.py:133
Sparse Core Ops, SparseCore 0:
  110.7 41.7 all-gather.5
  154.2 37.8 all-gather.3
  207.4 12.1 reduce-scatter.4
  222.4 58.2 reduce-scatter.2
  298.2 590.1 all-reduce.5
  890.6 28.4 all-reduce.7
